TPU v7x, 32 devices: a whole 2x2x4 slice. The times are simulated.
32 devices in a mesh: section: 16 (over z, y, core), seg: 2 (over x).
Axes of the slice: x: 2, y: 2, z: 4, core: 2. Of those that a mesh axis runs over, the one named last changes fastest.
Arguments:
- passage_word_codes: int32 [2, 256], P('seg'), may hold values from 0 to 16383
- word_vector_lookup: bfloat16 [16384, 2048], P('section'), may hold values from -6 to 6
- hidden_inputs: bfloat16 [2, 2048, 2048], P('seg', 'section'), may hold values from -6 to 6
- memory_blocks: bfloat16 [2, 2048, 2048], P('seg', 'section'), may hold values from -6 to 6
- asking_matrix: bfloat16 [16, 2048, 512], P('section'), may hold values from -0.125 to 0.125
- matching_matrix: bfloat16 [16, 2048, 512], P('section'), may hold values from -0.125 to 0.125
- content_matrix: bfloat16 [16, 2048, 512], P('section'), may hold values from -0.125 to 0.125
- projection_back_matrix: bfloat16 [16, 512, 2048], P('section'), may hold values from -0.75 to 0.75
- word_scale_factor: float32 [8, 2048], replicated, may hold values from 0.25 to 1.75
- memory_scale_factor: float32 [8, 2048], replicated, may hold values from 0.25 to 1.75
- memory_retention_share: float32 [8, 2048], replicated, may hold values from 0.1 to 0.9
- score_scaling: float32 [16, 4], P('section'), may hold values from 0.5 to 4, as said below
Outputs:
- hidden: bfloat16 [2, 2048, 2048], P('seg', 'section')
- new_states: bfloat16 [2, 2048, 2048], P('seg', 'section')
Inputs may be any that keep to these rules, and one draw needn't show every extreme that they name: `score_scaling`: positive score scales.
All inputs are finite; a program needn't handle non-finite values.
Results may differ from a plain program's by a relative error of at most 0.028.
The roundings to bfloat16 on the way count: a program that leaves them out, or rounds other values in their place, can miss the bound.
Values may be sent and summed in bfloat16 or wider, within the bound.
A program may use at most 64 MiB of HBM per device.

v0:
```python
import math

import jax
import jax.numpy as jnp
from jax import lax
from jax.sharding import PartitionSpec as P

HEAD_DIM = 128


def swapped(shard, axis, apart):
    return lax.ppermute(shard, axis, [(i, i ^ 1 << apart) for i in range(lax.axis_size(axis))])


def from_behind(value, axis, steps):
    count = lax.axis_size(axis)
    initial, last = (max(0, -steps), min(count, count - steps))
    return lax.ppermute(value, axis, [(source, source + steps) for source in range(initial, last)])


def passed_along(block, axis, distance):
    devices = range(lax.axis_size(axis))
    route = [((i - distance) % len(devices), i) for i in devices]
    return lax.ppermute(block, axis, route)


def norm_rows(values, gain_row):
    wide = values.astype(jnp.float32)
    meansq = jnp.mean(wide * wide, axis=-1, keepdims=True)
    return (wide * lax.rsqrt(meansq + 1e-06) * gain_row).astype(jnp.bfloat16)


def head_partial(
    word_lines,
    carried_memory,
    tok_gain,
    st_gain,
    proj_query,
    proj_key,
    proj_value,
    proj_out,
    scratch_numbers,
    head_dim,
):
    rescaled_lines = jnp.concatenate(
        [norm_rows(carried_memory, st_gain), norm_rows(word_lines, tok_gain)], axis=0
    )
    row_count = rescaled_lines.shape[0]
    state_count = carried_memory.shape[0]
    head_count = proj_query.shape[1] // head_dim
    queries = (
        jnp.dot(rescaled_lines, proj_query, preferred_element_type=jnp.float32)
        .astype(jnp.bfloat16)
        .reshape(row_count, head_count, head_dim)
    )
    key_rows = (
        jnp.dot(rescaled_lines, proj_key, preferred_element_type=jnp.float32)
        .astype(jnp.bfloat16)
        .reshape(row_count, head_count, head_dim)
    )
    value_rows = (
        jnp.dot(rescaled_lines, proj_value, preferred_element_type=jnp.float32)
        .astype(jnp.bfloat16)
        .reshape(row_count, head_count, head_dim)
    )
    scores = jnp.einsum("qhd,khd->hqk", queries, key_rows, preferred_element_type=jnp.float32)
    scaled = scores * (scratch_numbers / math.sqrt(head_dim))[:, None, None]
    query_pos = lax.iota(jnp.int32, row_count)[:, None]
    key_pos = lax.iota(jnp.int32, row_count)[None, :]
    allowed = (key_pos < state_count) | (query_pos < state_count) | (key_pos <= query_pos)
    masked = jnp.where(allowed[None], scaled, -jnp.inf)
    row_peak = jnp.max(masked, axis=-1, keepdims=True)
    exponent = jnp.exp(masked - row_peak)
    weights = (exponent / jnp.sum(exponent, axis=-1, keepdims=True)).astype(jnp.bfloat16)
    mixed_heads = jnp.einsum(
        "hqk,khd->qhd", weights, value_rows, preferred_element_type=jnp.float32
    )
    mixed_heads = mixed_heads.astype(jnp.bfloat16).reshape(row_count, head_count * head_dim)
    return jnp.dot(mixed_heads, proj_out, preferred_element_type=jnp.float32).astype(jnp.bfloat16)


def pair_join(mine, partner, pair_half):
    ordered = jnp.concatenate([mine, partner], axis=0)
    flipped = jnp.concatenate([partner, mine], axis=0)
    return jnp.where(pair_half == 0, ordered, flipped)


def assemble(tok_half, st_half, pair_half):
    other_tok, other_st = swapped((tok_half, st_half), "section", 0)
    return (pair_join(tok_half, other_tok, pair_half), pair_join(st_half, other_st, pair_half))


def reduce_half(partial_value, tok_half, st_half, pair_half, retain):
    st_size = st_half.shape[0]
    tok_size = tok_half.shape[0]
    partner = 1 - pair_half
    send_st = lax.dynamic_slice_in_dim(partial_value, partner * st_size, st_size, 0)
    send_tok = lax.dynamic_slice_in_dim(
        partial_value, 2 * st_size + partner * tok_size, tok_size, 0
    )
    got_st, got_tok = swapped((send_st, send_tok), "section", 0)
    own_st = lax.dynamic_slice_in_dim(partial_value, pair_half * st_size, st_size, 0)
    own_tok = lax.dynamic_slice_in_dim(
        partial_value, 2 * st_size + pair_half * tok_size, tok_size, 0
    )
    st_sum = own_st.astype(jnp.float32) + got_st.astype(jnp.float32)
    tok_sum = own_tok.astype(jnp.float32) + got_tok.astype(jnp.float32)
    tok_next = (tok_half.astype(jnp.float32) + tok_sum).astype(jnp.bfloat16)
    st_next = (retain * st_half.astype(jnp.float32) + (1.0 - retain) * st_sum).astype(jnp.bfloat16)
    return (tok_next, st_next)


def per_device(
    passage_word_codes,
    word_vector_lookup,
    hidden_inputs,
    memory_blocks,
    asking_matrix,
    matching_matrix,
    content_matrix,
    projection_back_matrix,
    word_scale_factor,
    memory_scale_factor,
    memory_retention_share,
    score_scaling,
):
    position = lax.axis_index("section")
    depth_level = position // 2
    pair_half = position % 2
    tok_gain = lax.dynamic_index_in_dim(word_scale_factor, depth_level, 0, keepdims=False)
    st_gain = lax.dynamic_index_in_dim(memory_scale_factor, depth_level, 0, keepdims=False)
    retain = lax.dynamic_index_in_dim(memory_retention_share, depth_level, 0, keepdims=False)
    proj_query = asking_matrix[0]
    proj_key = matching_matrix[0]
    proj_value = content_matrix[0]
    proj_out = projection_back_matrix[0]
    scratch_numbers = score_scaling[0]
    head_dim = HEAD_DIM
    tok_half = hidden_inputs[0]
    st_half = memory_blocks[0]
    tok_size = tok_half.shape[0]
    vocab_dev = word_vector_lookup.shape[0]
    codes = vocab_dev * position + lax.iota(jnp.int32, vocab_dev)
    onehot = (passage_word_codes[0][:, None] == codes[None, :]).astype(jnp.bfloat16)
    looked = jnp.dot(onehot, word_vector_lookup, preferred_element_type=jnp.float32)
    embedded = lax.psum(looked, "section").astype(jnp.bfloat16)
    tok_full, st_full = assemble(tok_half, st_half, pair_half)
    partial_value = head_partial(
        tok_full,
        st_full,
        tok_gain,
        st_gain,
        proj_query,
        proj_key,
        proj_value,
        proj_out,
        scratch_numbers,
        head_dim,
    )
    tok_next, st_next = reduce_half(partial_value, tok_half, st_half, pair_half, retain)
    moved_tok = from_behind(tok_next, "section", 2)
    emb_half = lax.dynamic_slice_in_dim(embedded, pair_half * tok_size, tok_size, 0)
    tok_second = jnp.where(depth_level == 0, emb_half, moved_tok)
    st_second = passed_along(st_next, "seg", 1)
    tok_full2, st_full2 = assemble(tok_second, st_second, pair_half)
    partial_two = head_partial(
        tok_full2,
        st_full2,
        tok_gain,
        st_gain,
        proj_query,
        proj_key,
        proj_value,
        proj_out,
        scratch_numbers,
        head_dim,
    )
    tok_final, st_final = reduce_half(partial_two, tok_second, st_second, pair_half, retain)
    return (tok_final[None], st_final[None])


def solution(mesh):
    placed = (
        P("seg", None),
        P("section", None),
        P("seg", "section", None),
        P("seg", "section", None),
        P("section", None, None),
        P("section", None, None),
        P("section", None, None),
        P("section", None, None),
        P(),
        P(),
        P(),
        P("section", None),
    )
    return jax.shard_map(
        per_device,
        mesh=mesh,
        in_specs=placed,
        out_specs=(P("seg", "section", None), P("seg", "section", None)),
        check_vma=False,
    )
```

profile of v0, /device:TPU:0, one launch (start us, length us, event | category | flops | bytes accessed | tf_op | source)
XLA Modules:
  0.0 153.9 jit_solution(3155172350396124642)
XLA Ops:
  3.9 3.1 %fusion.4 = (f32[256]{0:T(256)S(1)}, f32[256]{0:T(256)S(1)}) fusion(bf16[128,2048]{1,0:T(8,128)(2,1)} %bitcast.73, bf16[128,2048]{1,0:T(8,128)(2,1)} %collective-permute-done, pred[]{:T(512)S(6)} %eq.31, bf16[128,2048]{1,0:T(8,128)(2,1)} %bitcast.76, bf16[128,2048]{1,0:T(8,128)(2,1)} %collective-permute-done.1), kind=kLoop, calls=%fused_computation.20 | loop fusion | flops 12582400 | bytes 2099201 | tf_op jit(solution)/shard_map/reduce_sum | solution.py:29
  7.0 1.9 %fusion.9 = bf16[256,2048]{1,0:T(8,128)(2,1)S(1)} fusion(f32[2048]{0:T(1024)S(1)} %bitcast.82, f32[256]{0:T(256)S(1)} %add_rsqrt_fusion.2, bf16[128,2048]{1,0:T(8,128)(2,1)S(1)} %bitcast.77, bf16[128,2048]{1,0:T(8,128)(2,1)} %collective-permute-done.1, pred[]{:T(512)S(6)} %eq.31), kind=kLoop, calls=%fused_computation.25 | loop fusion | flops 6815744 | bytes 2106369 | tf_op jit(solution)/shard_map/convert_element_type | solution.py:30
  8.9 1.7 %fusion.6 = bf16[256,2048]{1,0:T(8,128)(2,1)S(1)} fusion(f32[2048]{0:T(1024)S(1)} %bitcast.84, f32[256]{0:T(256)S(1)} %add_rsqrt_fusion.3, bf16[128,2048]{1,0:T(8,128)(2,1)S(1)} %bitcast.74, bf16[128,2048]{1,0:T(8,128)(2,1)} %collective-permute-done, pred[]{:T(512)S(6)} %eq.31), kind=kLoop, calls=%fused_computation.22 | loop fusion | flops 6815744 | bytes 2106369 | tf_op jit(solution)/shard_map/convert_element_type | solution.py:30
  10.7 2.1 %fusion.38 = bf16[512,512]{0,1:T(8,128)(2,1)} fusion(bf16[1,2048,512]{2,1,0:T(8,128)(2,1)S(1)} %copy-done.5, bf16[256,2048]{1,0:T(8,128)(2,1)S(1)} %fusion.9, bf16[256,2048]{1,0:T(8,128)(2,1)S(1)} %fusion.6), kind=kOutput, calls=%fused_computation.56 | convolution fusion | flops 1078198272 | bytes 4718592 | tf_op jit(solution)/shard_map/dot_general | solution.py:62
  12.8 2.1 %fusion.44 = bf16[512,512]{0,1:T(8,128)(2,1)} fusion(bf16[1,2048,512]{2,1,0:T(8,128)(2,1)S(1)} %copy-done.7, bf16[256,2048]{1,0:T(8,128)(2,1)S(1)} %fusion.9, bf16[256,2048]{1,0:T(8,128)(2,1)S(1)} %fusion.6), kind=kOutput, calls=%fused_computation.58 | convolution fusion | flops 1078198272 | bytes 4718592 | tf_op jit(solution)/shard_map/dot_general | solution.py:52
  14.8 2.1 %fusion.50 = bf16[512,512]{0,1:T(8,128)(2,1)} fusion(bf16[1,2048,512]{2,1,0:T(8,128)(2,1)S(1)} %copy-done.9, bf16[256,2048]{1,0:T(8,128)(2,1)S(1)} %fusion.9, bf16[256,2048]{1,0:T(8,128)(2,1)S(1)} %fusion.6), kind=kOutput, calls=%fused_computation.60 | convolution fusion | flops 1078198272 | bytes 4718592 | tf_op jit(solution)/shard_map/dot_general | solution.py:57
  16.9 4.9 %fusion.78 = (f32[4,512]{1,0:T(4,128)S(1)}, f32[4,512,512]{1,2,0:T(8,128)}) fusion(f32[4]{0:T(128)S(1)} %multiply_bitcast_fusion, pred[512,512]{0,1:T(8,128)(4,1)S(1)} %fusion.58, bf16[512,4,128]{0,2,1:T(8,128)(2,1)} %bitcast.91, bf16[512,4,128]{0,2,1:T(8,128)(2,1)} %bitcast.92), kind=kOutput, calls=%fused_computation.107 | convolution fusion | flops 272630272 | bytes 5513232 | tf_op jit(solution)/shard_map/sub | solution.py:73
  21.8 2.8 %fusion.57 = bf16[4,128,512]{2,1,0:T(8,128)(2,1)S(1)} fusion(bf16[512,4,128]{0,2,1:T(8,128)(2,1)} %bitcast.88, f32[4,512,512]{1,2,0:T(8,128)} %get-tuple-element.13, f32[4,512]{1,0:T(4,128)S(1)} %get-tuple-element.12), kind=kOutput, calls=%fused_computation.63 | convolution fusion | flops 270794752 | bytes 5251072 | tf_op jit(solution)/shard_map/hqk,khd->qhd/dot_general | solution.py:75
  24.6 1.3 convolution_convert_fusion.1
  25.9 1.3 copy-done.3
  28.8 2.7 %fusion.59 = f32[256,2048]{1,0:T(8,128)} fusion(bf16[1024,2048]{1,0:T(8,128)(2,1)S(1)} %copy-done.4, s32[1024]{0:T(1024)S(1)} %iota_add_fusion, s32[256]{0:T(256)S(1)} %bitcast.86), kind=kOutput, calls=%fused_computation.75 | convolution fusion | flops 1074003968 | bytes 6296576 | tf_op jit(solution)/shard_map/dot_general | solution.py:145
  32.3 3.0 %add_convert_fusion.2 = (bf16[128,2048]{1,0:T(8,128)(2,1)}, bf16[128,2048]{1,0:T(8,128)(2,1)}) fusion(bf16[128,2048]{1,0:T(8,128)(2,1)} %collective-permute-done.4, bf16[512,2048]{1,0:T(8,128)(2,1)} %copy-done.3, s32[]{:T(128)S(6)} %select_n.83, f32[2048]{0:T(1024)S(1)} %bitcast.78, f32[2048]{0:T(1024)S(1)} %bitcast.80, ...), kind=kLoop, calls=%fused_computation.71 | loop fusion | flops 3670016 | bytes 4210696 | tf_op jit(solution)/shard_map/convert_element_type | solution.py:109
  35.4 5.6 %collective-permute-start.3 = (bf16[128,2048]{1,0:T(8,128)(2,1)}, bf16[128,2048]{1,0:T(8,128)(2,1)}, u32[]{:S(2)}, u32[]{:S(2)}) collective-permute-start(bf16[128,2048]{1,0:T(8,128)(2,1)} %get-tuple-element.9), channel_id=1, source_target_pairs={{0,4},{2,6},{4,8},{6,10},{8,12},{10,14},{12,16},{14,18},{16,20},{1... | collective-permute-start | bytes 1572872 | tf_op jit(solution)/shard_map/ppermute | solution.py:18
  41.0 79.4 %all-reduce.1 = bf16[256,2048]{1,0:T(8,128)(2,1)} all-reduce(f32[256,2048]{1,0:T(8,128)} %fusion.59), channel_id=1, replica_groups=mesh['section'=16,'seg'=2] {'section'}, use_global_device_ids=true, to_apply=%region_0.1 | all-reduce | flops 524288 | bytes 3145728 | tf_op jit(solution)/shard_map/psum | solution.py:146
  120.4 1.5 collective-permute-start.5
  123.1 7.3 %collective-permute-done.5 = bf16[128,2048]{1,0:T(8,128)(2,1)S(1)} collective-permute-done((bf16[128,2048]{1,0:T(8,128)(2,1)}, bf16[128,2048]{1,0:T(8,128)(2,1)S(1)}, u32[]{:S(2)}, u32[]{:S(2)}) %collective-permute-start.5) | collective-permute-done | bytes 524320 | tf_op jit(solution)/shard_map/ppermute | solution.py:24
  130.8 1.5 %collective-permute-done.6 = bf16[128,2048]{1,0:T(8,128)(2,1)S(1)} collective-permute-done((bf16[128,2048]{1,0:T(8,128)(2,1)S(1)}, bf16[128,2048]{1,0:T(8,128)(2,1)S(1)}, u32[]{:S(2)}, u32[]{:S(2)}) %collective-permute-start.6) | collective-permute-done | bytes 524320 | tf_op jit(solution)/shard_map/ppermute | solution.py:12
  134.3 2.1 %fusion.41 = bf16[512,512]{0,1:T(8,128)(2,1)} fusion(bf16[1,2048,512]{2,1,0:T(8,128)(2,1)S(1)} %copy-done.6, bf16[256,2048]{1,0:T(8,128)(2,1)S(1)} %fusion.15, bf16[256,2048]{1,0:T(8,128)(2,1)S(1)} %fusion.12), kind=kOutput, calls=%fused_computation.57 | convolution fusion | flops 1078198272 | bytes 4718592 | tf_op jit(solution)/shard_map/dot_general | solution.py:62
  136.4 2.1 %fusion.47 = bf16[512,512]{0,1:T(8,128)(2,1)} fusion(bf16[1,2048,512]{2,1,0:T(8,128)(2,1)S(1)} %copy-done.8, bf16[256,2048]{1,0:T(8,128)(2,1)S(1)} %fusion.15, bf16[256,2048]{1,0:T(8,128)(2,1)S(1)} %fusion.12), kind=kOutput, calls=%fused_computation.59 | convolution fusion | flops 1078198272 | bytes 4718592 | tf_op jit(solution)/shard_map/dot_general | solution.py:52
  138.5 2.1 %fusion.53 = bf16[512,512]{0,1:T(8,128)(2,1)} fusion(bf16[1,2048,512]{2,1,0:T(8,128)(2,1)S(1)} %copy-done.10, bf16[256,2048]{1,0:T(8,128)(2,1)S(1)} %fusion.15, bf16[256,2048]{1,0:T(8,128)(2,1)S(1)} %fusion.12), kind=kOutput, calls=%fused_computation.61 | convolution fusion | flops 1078198272 | bytes 4718592 | tf_op jit(solution)/shard_map/dot_general | solution.py:57
  140.6 4.9 %fusion.79 = (f32[4,512]{1,0:T(4,128)S(1)}, f32[4,512,512]{1,2,0:T(8,128)}) fusion(f32[4]{0:T(128)S(1)} %multiply_bitcast_fusion, pred[512,512]{0,1:T(8,128)(4,1)S(1)} %fusion.58, bf16[512,4,128]{0,2,1:T(8,128)(2,1)} %bitcast.89, bf16[512,4,128]{0,2,1:T(8,128)(2,1)} %bitcast.90), kind=kOutput, calls=%fused_computation.108 | convolution fusion | flops 272630272 | bytes 5513232 | tf_op jit(solution)/shard_map/sub | solution.py:73
  145.4 2.8 %fusion.56 = bf16[4,128,512]{2,1,0:T(8,128)(2,1)S(1)} fusion(bf16[512,4,128]{0,2,1:T(8,128)(2,1)} %bitcast.87, f32[4,512,512]{1,2,0:T(8,128)} %get-tuple-element.15, f32[4,512]{1,0:T(4,128)S(1)} %get-tuple-element.14), kind=kOutput, calls=%fused_computation.62 | convolution fusion | flops 270794752 | bytes 5251072 | tf_op jit(solution)/shard_map/hqk,khd->qhd/dot_general | solution.py:75
  150.2 1.4 collective-permute-done.9
  152.4 1.5 fusion.62
  (57 shorter events, 11.9 us)
Async XLA Ops:
  0.6 24.0 %copy-start = (bf16[1,512,2048]{2,1,0:T(8,128)(2,1)S(1)}, bf16[1,512,2048]{2,1,0:T(8,128)(2,1)}, u32[]{:S(2)}) copy-start(bf16[1,512,2048]{2,1,0:T(8,128)(2,1)} %param.19) | copy-start | bytes 6291460
  0.6 6.4 %copy-start.2 = (bf16[1,128,2048]{2,1,0:T(8,128)(2,1)S(1)}, bf16[1,128,2048]{2,1,0:T(8,128)(2,1)}, u32[]{:S(2)}) copy-start(bf16[1,128,2048]{2,1,0:T(8,128)(2,1)} %param.14) | copy-start | bytes 1572868
  0.7 3.2 %collective-permute-start = (bf16[128,2048]{1,0:T(8,128)(2,1)}, bf16[128,2048]{1,0:T(8,128)(2,1)}, u32[]{:S(2)}, u32[]{:S(2)}) collective-permute-start(bf16[128,2048]{1,0:T(8,128)(2,1)} %bitcast.72), channel_id=1, source_target_pairs={{0,2},{2,0},{4,6},{6,4},{8,10},{10,8},{12,14},{14,12},{16,18},{18,... | collective-permute-start | bytes 1572872 | tf_op jit(solution)/shard_map/ppermute | solution.py:12
  1.2 2.7 %collective-permute-start.1 = (bf16[128,2048]{1,0:T(8,128)(2,1)}, bf16[128,2048]{1,0:T(8,128)(2,1)}, u32[]{:S(2)}, u32[]{:S(2)}) collective-permute-start(bf16[128,2048]{1,0:T(8,128)(2,1)} %bitcast.75), channel_id=1, source_target_pairs={{0,2},{2,0},{4,6},{6,4},{8,10},{10,8},{12,14},{14,12},{16,18},{18,... | collective-permute-start | bytes 1572872 | tf_op jit(solution)/shard_map/ppermute | solution.py:12
  3.9 5.0 %copy-start.1 = (bf16[1,128,2048]{2,1,0:T(8,128)(2,1)S(1)}, bf16[1,128,2048]{2,1,0:T(8,128)(2,1)}, u32[]{:S(2)}) copy-start(bf16[1,128,2048]{2,1,0:T(8,128)(2,1)} %param.15) | copy-start | bytes 1572868
  7.0 3.6 %copy-start.5 = (bf16[1,2048,512]{2,1,0:T(8,128)(2,1)S(1)}, bf16[1,2048,512]{2,1,0:T(8,128)(2,1)}, u32[]{:S(2)}) copy-start(bf16[1,2048,512]{2,1,0:T(8,128)(2,1)} %param.18) | copy-start | bytes 6291460
  10.6 2.1 %copy-start.7 = (bf16[1,2048,512]{2,1,0:T(8,128)(2,1)S(1)}, bf16[1,2048,512]{2,1,0:T(8,128)(2,1)}, u32[]{:S(2)}) copy-start(bf16[1,2048,512]{2,1,0:T(8,128)(2,1)} %param.16) | copy-start | bytes 6291460
  12.8 2.1 %copy-start.9 = (bf16[1,2048,512]{2,1,0:T(8,128)(2,1)S(1)}, bf16[1,2048,512]{2,1,0:T(8,128)(2,1)}, u32[]{:S(2)}) copy-start(bf16[1,2048,512]{2,1,0:T(8,128)(2,1)} %param.17) | copy-start | bytes 6291460
  24.6 4.2 %copy-start.4 = (bf16[1024,2048]{1,0:T(8,128)(2,1)S(1)}, bf16[1024,2048]{1,0:T(8,128)(2,1)}, u32[]{:S(2)}) copy-start(bf16[1024,2048]{1,0:T(8,128)(2,1)} %param.13) | copy-start | bytes 12582916
  25.9 1.3 copy-start.3
  27.2 1.6 %copy-start.11 = (s32[1,256]{1,0:T(1,128)S(1)}, s32[1,256]{1,0:T(1,128)}, u32[]{:S(2)}) copy-start(s32[1,256]{1,0:T(1,128)} %param.12) | copy-start | bytes 3076
  28.3 4.1 %collective-permute-start.4 = (bf16[128,2048]{1,0:T(8,128)(2,1)}, bf16[128,2048]{1,0:T(8,128)(2,1)}, u32[]{:S(2)}, u32[]{:S(2)}) collective-permute-start(bf16[128,2048]{1,0:T(8,128)(2,1)} %get-tuple-element.10), channel_id=1, source_target_pairs={{0,2},{2,0},{4,6},{6,4},{8,10},{10,8},{12,14},{14,12},{16,18},{18,... | collective-permute-start | bytes 1572872 | tf_op jit(solution)/shard_map/ppermute | solution.py:12
  28.7 3.7 %collective-permute-start.2 = (bf16[128,2048]{1,0:T(8,128)(2,1)}, bf16[128,2048]{1,0:T(8,128)(2,1)}, u32[]{:S(2)}, u32[]{:S(2)}) collective-permute-start(bf16[128,2048]{1,0:T(8,128)(2,1)} %get-tuple-element.11), channel_id=1, source_target_pairs={{0,2},{2,0},{4,6},{6,4},{8,10},{10,8},{12,14},{14,12},{16,18},{18,... | collective-permute-start | bytes 1572872 | tf_op jit(solution)/shard_map/ppermute | solution.py:12
  35.4 86.5 %collective-permute-start.3 = (bf16[128,2048]{1,0:T(8,128)(2,1)}, bf16[128,2048]{1,0:T(8,128)(2,1)}, u32[]{:S(2)}, u32[]{:S(2)}) collective-permute-start(bf16[128,2048]{1,0:T(8,128)(2,1)} %get-tuple-element.9), channel_id=1, source_target_pairs={{0,4},{2,6},{4,8},{6,10},{8,12},{10,14},{12,16},{14,18},{16,20},{1... | collective-permute-start | bytes 1572872 | tf_op jit(solution)/shard_map/ppermute | solution.py:18
  120.4 10.1 %collective-permute-start.5 = (bf16[128,2048]{1,0:T(8,128)(2,1)}, bf16[128,2048]{1,0:T(8,128)(2,1)S(1)}, u32[]{:S(2)}, u32[]{:S(2)}) collective-permute-start(bf16[128,2048]{1,0:T(8,128)(2,1)} %get-tuple-element.8), channel_id=1, source_target_pairs={{1,0},{0,1},{3,2},{2,3},{5,4},{4,5},{7,6},{6,7},{9,8},{8,9},{11,10... | collective-permute-start | bytes 1572872 | tf_op jit(solution)/shard_map/ppermute | solution.py:24
  123.0 7.4 %collective-permute-start.7 = (bf16[128,2048]{1,0:T(8,128)(2,1)S(1)}, bf16[128,2048]{1,0:T(8,128)(2,1)S(1)}, u32[]{:S(2)}, u32[]{:S(2)}) collective-permute-start(bf16[128,2048]{1,0:T(8,128)(2,1)S(1)} %fusion.63), channel_id=1, source_target_pairs={{0,2},{2,0},{4,6},{6,4},{8,10},{10,8},{12,14},{14,12},{16,18},{18,... | collective-permute-start | bytes 1572872 | tf_op jit(solution)/shard_map/ppermute | solution.py:12
  130.4 1.9 %collective-permute-start.6 = (bf16[128,2048]{1,0:T(8,128)(2,1)S(1)}, bf16[128,2048]{1,0:T(8,128)(2,1)S(1)}, u32[]{:S(2)}, u32[]{:S(2)}) collective-permute-start(bf16[128,2048]{1,0:T(8,128)(2,1)S(1)} %collective-permute-done.5), channel_id=1, source_target_pairs={{0,2},{2,0},{4,6},{6,4},{8,10},{10,8},{12,14},{14,12},{16,18},{18,... | collective-permute-start | bytes 1572872 | tf_op jit(solution)/shard_map/ppermute | solution.py:12
  132.7 1.6 %copy-start.6 = (bf16[1,2048,512]{2,1,0:T(8,128)(2,1)S(1)}, bf16[1,2048,512]{2,1,0:T(8,128)(2,1)}, u32[]{:S(2)}) copy-start(bf16[1,2048,512]{2,1,0:T(8,128)(2,1)} %param.18) | copy-start | bytes 6291460
  134.3 2.1 %copy-start.8 = (bf16[1,2048,512]{2,1,0:T(8,128)(2,1)S(1)}, bf16[1,2048,512]{2,1,0:T(8,128)(2,1)}, u32[]{:S(2)}) copy-start(bf16[1,2048,512]{2,1,0:T(8,128)(2,1)} %param.16) | copy-start | bytes 6291460
  136.4 2.1 %copy-start.10 = (bf16[1,2048,512]{2,1,0:T(8,128)(2,1)S(1)}, bf16[1,2048,512]{2,1,0:T(8,128)(2,1)}, u32[]{:S(2)}) copy-start(bf16[1,2048,512]{2,1,0:T(8,128)(2,1)} %param.17) | copy-start | bytes 6291460
  149.6 2.0 %collective-permute-start.9 = (bf16[128,2048]{1,0:T(8,128)(2,1)S(1)}, bf16[128,2048]{1,0:T(8,128)(2,1)S(1)}, u32[]{:S(2)}, u32[]{:S(2)}) collective-permute-start(bf16[128,2048]{1,0:T(8,128)(2,1)S(1)} %get-tuple-element.6), channel_id=1, source_target_pairs={{0,2},{2,0},{4,6},{6,4},{8,10},{10,8},{12,14},{14,12},{16,18},{18,... | collective-permute-start | bytes 1572872 | tf_op jit(solution)/shard_map/ppermute | solution.py:12
  149.8 2.5 %collective-permute-start.8 = (bf16[128,2048]{1,0:T(8,128)(2,1)S(1)}, bf16[128,2048]{1,0:T(8,128)(2,1)S(1)}, u32[]{:S(2)}, u32[]{:S(2)}) collective-permute-start(bf16[128,2048]{1,0:T(8,128)(2,1)S(1)} %get-tuple-element.7), channel_id=1, source_target_pairs={{0,2},{2,0},{4,6},{6,4},{8,10},{10,8},{12,14},{14,12},{16,18},{18,... | collective-permute-start | bytes 1572872 | tf_op jit(solution)/shard_map/ppermute | solution.py:12
where the time goes:
time: 154 us
  blocking collectives  79.4 us (52%)
  matrix products  33.1 us (21%)
  other arithmetic  15.9 us (10%)
  waiting for transfers between devices  11 us (7%)
  starting transfers between devices  8.86 us (6%)
  local copies, waits for them, and re-layouts  4.7 us (3%)
    psum x1, blocking collectives, per_device(): embedded = lax.psum(looked, 'section').astype(jnp.bfloat16)  79.4 us
    sub x2, matrix products, head_partial(): exponent = jnp.exp(masked - row_peak)  9.72 us
    ppermute x1, waiting for transfers between devices, passed_along(): return lax.ppermute(block, axis, route)  7.34 us
    dot_general x2, matrix products, head_partial(): jnp.einsum('hqk,khd->qhd', weights, value_rows, preferred_element_type=jn...  5.62 us
    ppermute x1, starting transfers between devices, from_behind(): lax.ppermute(value, axis, [(source, source + steps) for source in range(i...  5.62 us
    convert_element_type x4, other arithmetic, norm_rows(): return (wide * lax.rsqrt(meansq + 1e-06) * gain_row).astype(jnp.bfloat16)  4.64 us
    dot_general x2, matrix products, head_partial(): jnp.dot(rescaled_lines, proj_key, preferred_element_type=jnp.float32)  4.19 us
    dot_general x2, matrix products, head_partial(): jnp.dot(rescaled_lines, proj_value, preferred_element_type=jnp.float32)  4.17 us
  transfers between devices with their start and end apart: 10, of which 4 were waited for; matrix products, arithmetic and copies ran while one was open for 5% of the time, Pallas kernels for 0%

commit v1 on v0

v1 whole, which is shorter than its diff:
```python
import functools
import math

import jax
import jax.numpy as jnp
from jax import lax
from jax.experimental import pallas as pl
from jax.experimental.pallas import tpu as pltpu
from jax.sharding import PartitionSpec as P

HEAD_DIM = 128
LOG2E = math.log2(math.e)
F32 = jnp.float32
BF16 = jnp.bfloat16
MESH = pl.DeviceIdType.MESH


def cell_kernel(
    n_layers,
    n_seg,
    codes_hbm,
    table_hbm,
    tok_hbm,
    st_hbm,
    wq_hbm,
    wk_hbm,
    wv_hbm,
    wo_hbm,
    wgain_hbm,
    mgain_hbm,
    keep_hbm,
    scale_ref,
    tok_out,
    st_out,
    codes,
    table,
    x1,
    c1,
    wq,
    wk,
    wv,
    wo,
    wgain,
    mgain,
    keep,
    onehot,
    emb_own,
    emb_send,
    emb_got,
    a2a,
    emb_red,
    u1,
    u2,
    q,
    k,
    v,
    o1,
    o2,
    ost,
    x2,
    c2,
    y1,
    s2,
    part_send1,
    part_got1,
    part_send2,
    part_got2,
    part_send3,
    part_got3,
    part_send4,
    part_got4,
    fin_tok,
    fin_st,
    load_sem,
    pair_send,
    pair_recv,
    a2a_send,
    a2a_recv,
    red_send,
    red_recv,
    seg_send,
    seg_recv,
    tok_send,
    tok_recv,
    out_sem,
):
    pos = lax.axis_index("section")
    seg = lax.axis_index("seg")
    layer = pos // 2
    half = pos % 2
    mate = layer * 2 + (1 - half)
    seg_next = lax.rem(seg + 1, n_seg)
    seg_prev = lax.rem(seg + n_seg - 1, n_seg)
    rows = x1.shape[0]
    width = x1.shape[1]
    chunk = width // n_layers
    heads = wq.shape[1] // HEAD_DIM

    barrier = pltpu.get_barrier_semaphore()
    pl.semaphore_signal(barrier, inc=1, device_id={"section": mate}, device_id_type=MESH)
    for other in (seg_next, seg_prev):
        pl.semaphore_signal(barrier, inc=1, device_id={"seg": other}, device_id_type=MESH)

    @pl.loop(1, n_layers)
    def _(step):
        peer = lax.rem(layer + step, n_layers) * 2 + half
        pl.semaphore_signal(barrier, inc=1, device_id={"section": peer}, device_id_type=MESH)

    pairs = (
        (st_hbm, c1),
        (tok_hbm, x1),
        (mgain_hbm, mgain),
        (wgain_hbm, wgain),
        (codes_hbm, codes),
        (table_hbm, table),
        (wq_hbm, wq),
        (wk_hbm, wk),
        (wv_hbm, wv),
        (keep_hbm, keep),
        (wo_hbm, wo),
    )
    loads = [pltpu.make_async_copy(a, b, load_sem.at[i]) for i, (a, b) in enumerate(pairs)]
    for load in loads:
        load.start()

    def norm_into(src, gain_ref, dst, base):
        gain = gain_ref[pl.ds(layer, 1), :]

        @pl.loop(0, rows // 16)
        def _(i):
            r = pl.multiple_of(i * 16, 16)
            wide = src[pl.ds(r, 16), :].astype(F32)
            meansq = jnp.mean(wide * wide, axis=-1, keepdims=True)
            dst[pl.ds(base + r, 16), :] = (wide * lax.rsqrt(meansq + 1e-06) * gain).astype(BF16)

    def to_mate(src, dst, i):
        return pltpu.make_async_remote_copy(
            src_ref=src,
            dst_ref=dst,
            send_sem=pair_send.at[i],
            recv_sem=pair_recv.at[i],
            device_id={"section": mate},
            device_id_type=MESH,
        )

    def to_seg(src, dst, i):
        return pltpu.make_async_remote_copy(
            src_ref=src,
            dst_ref=dst,
            send_sem=seg_send.at[i],
            recv_sem=seg_recv.at[i],
            device_id={"seg": seg_next},
            device_id_type=MESH,
        )

    def project(u, base):
        block = u[pl.ds(base, 2 * rows), :]
        for w, dst in ((wq, q), (wk, k), (wv, v)):
            dst[pl.ds(base, 2 * rows), :] = jnp.dot(
                block, w[...], preferred_element_type=F32
            ).astype(BF16)

    def attend(o, first, masked):
        @pl.loop(0, 2)
        def _(b):
            base = pl.multiple_of(first + b * rows, rows)
            if masked:
                col = lax.broadcasted_iota(jnp.int32, (rows, 4 * rows), 1)
                row = lax.broadcasted_iota(jnp.int32, (rows, 4 * rows), 0)
                own = half * rows
                far = (1 - half) * rows
                kpos = jnp.where(
                    col < 2 * rows,
                    -1,
                    jnp.where(col < 3 * rows, col - 2 * rows + own, col - 3 * rows + far),
                )
                qpos = row + (own + b * (far - own))
                allowed = kpos <= qpos
            for h in range(heads):
                lanes = pl.ds(h * HEAD_DIM, HEAD_DIM)
                s = lax.dot_general(
                    q[pl.ds(base, rows), lanes],
                    k[:, lanes],
                    (((1,), (1,)), ((), ())),
                    preferred_element_type=F32,
                )
                s = s * (scale_ref[0, h] * (LOG2E / math.sqrt(HEAD_DIM)))
                if masked:
                    s = jnp.where(allowed, s, -jnp.inf)
                e = jnp.exp2(s - jnp.max(s, axis=-1, keepdims=True))
                p = (e * (1.0 / jnp.sum(e, axis=-1, keepdims=True))).astype(BF16)
                o[pl.ds(base, rows), lanes] = jnp.dot(
                    p, v[:, lanes], preferred_element_type=F32
                ).astype(BF16)

    def back(o, base, dst):
        dst[...] = jnp.dot(
            o[pl.ds(base, rows), :], wo[...], preferred_element_type=F32
        ).astype(BF16)

    def token_sum(o, base, x, got, dst):
        @pl.loop(0, width // 512)
        def _(t):
            cols = pl.ds(pl.multiple_of(t * 512, 512), 512)
            mine = jnp.dot(
                o[pl.ds(base, rows), :], wo[:, cols], preferred_element_type=F32
            ).astype(BF16)
            total = mine.astype(F32) + got[:, cols].astype(F32)
            dst[:, cols] = (x[:, cols].astype(F32) + total).astype(BF16)

    def state_sum(o, base, c, got, dst):
        @pl.loop(0, width // 512)
        def _(t):
            cols = pl.ds(pl.multiple_of(t * 512, 512), 512)
            mine = jnp.dot(
                o[pl.ds(base, rows), :], wo[:, cols], preferred_element_type=F32
            ).astype(BF16)
            total = mine.astype(F32) + got[:, cols].astype(F32)
            r = keep[pl.ds(layer, 1), cols]
            dst[:, cols] = (r * c[:, cols].astype(F32) + (1.0 - r) * total).astype(BF16)

    loads[0].wait()
    loads[2].wait()
    norm_into(c1, mgain, u1, 0)
    loads[1].wait()
    loads[3].wait()
    norm_into(x1, wgain, u1, 2 * rows)
    pl.semaphore_wait(barrier, n_layers + 2)
    send_u1s = to_mate(u1.at[pl.ds(0, rows)], u1.at[pl.ds(rows, rows)], 0)
    send_u1s.start()
    send_u1t = to_mate(u1.at[pl.ds(2 * rows, rows)], u1.at[pl.ds(3 * rows, rows)], 1)
    send_u1t.start()
    send_c = to_seg(c1, c2, 0)
    send_c.start()

    loads[4].wait()
    vocab = table.shape[0]
    ids = jnp.broadcast_to(codes[...].astype(F32), (HEAD_DIM, 2 * rows)).T
    lane = lax.broadcasted_iota(jnp.int32, ids.shape, 1) + pos * vocab
    for b in range(vocab // HEAD_DIM):
        hit = ids == (lane + b * HEAD_DIM).astype(F32)
        onehot[:, b * HEAD_DIM : (b + 1) * HEAD_DIM] = jnp.where(hit, 1.0, 0.0).astype(BF16)
    loads[5].wait()
    own_rows = pl.ds(pl.multiple_of(half * rows, rows), rows)
    far_rows = pl.ds(pl.multiple_of((1 - half) * rows, rows), rows)

    @pl.loop(0, n_layers)
    def _(j):
        cols = pl.ds(pl.multiple_of(j * chunk, chunk), chunk)
        part = table[:, cols]
        emb_send[j] = jnp.dot(onehot[far_rows, :], part, preferred_element_type=F32).astype(BF16)
        emb_own[j] = jnp.dot(onehot[own_rows, :], part, preferred_element_type=F32).astype(BF16)

    send_emb = to_mate(emb_send, emb_got, 2)
    send_emb.start()

    send_u1s.wait_recv()
    loads[6].wait()
    loads[7].wait()
    loads[8].wait()
    project(u1, 0)

    send_emb.wait_recv()
    emb_own[...] = emb_own[...] + emb_got[...]

    def a2a_copy(step):
        peer = lax.rem(layer + step, n_layers)
        return pltpu.make_async_remote_copy(
            src_ref=emb_own.at[peer],
            dst_ref=a2a.at[layer],
            send_sem=a2a_send.at[peer],
            recv_sem=a2a_recv.at[layer],
            device_id={"section": peer * 2 + half},
            device_id_type=MESH,
        )

    def a2a_arrival(step):
        peer = lax.rem(layer + step, n_layers)
        return pltpu.make_async_remote_copy(
            src_ref=emb_own.at[layer],
            dst_ref=a2a.at[peer],
            send_sem=a2a_send.at[layer],
            recv_sem=a2a_recv.at[peer],
            device_id={"section": peer * 2 + half},
            device_id_type=MESH,
        )

    @pl.loop(1, n_layers)
    def _(step):
        a2a_copy(step).start()

    send_u1t.wait_recv()
    project(u1, 2 * rows)

    attend(o1, 2 * rows, True)
    loads[10].wait()
    back(o1, 3 * rows, part_send1)
    send_p1 = to_mate(part_send1, part_got1, 3)
    send_p1.start()
    send_p1.wait_recv()
    token_sum(o1, 2 * rows, x1, part_got1, y1)

    def token_copy(target):
        return pltpu.make_async_remote_copy(
            src_ref=y1,
            dst_ref=x2,
            send_sem=tok_send,
            recv_sem=tok_recv,
            device_id={"section": target},
            device_id_type=MESH,
        )

    last = n_layers - 1
    up = jnp.where(layer < last, pos + 2, pos - 2 * last)

    @pl.when(layer < last)
    def _():
        token_copy(up).start()

    attend(o1, 0, False)
    send_o = to_seg(o1.at[pl.ds(0, 2 * rows)], ost, 1)
    send_o.start()

    emb_red[...] = emb_own[layer]

    @pl.loop(1, n_layers)
    def _(step):
        a2a_arrival(step).wait_recv()
        emb_red[...] = emb_red[...] + a2a[lax.rem(layer + step, n_layers)]

    my_cols = pl.ds(pl.multiple_of(layer * chunk, chunk), chunk)

    def red_copy():
        return pltpu.make_async_remote_copy(
            src_ref=emb_red,
            dst_ref=x2.at[:, my_cols],
            send_sem=red_send,
            recv_sem=red_recv.at[layer],
            device_id={"section": half},
            device_id_type=MESH,
        )

    @pl.when(layer > 0)
    def _():
        red_copy().start()

    send_o.wait_recv()
    back(ost, rows, part_send2)
    send_p2 = to_mate(part_send2, part_got2, 4)
    send_p2.start()
    send_c.wait_recv()
    loads[9].wait()
    send_p2.wait_recv()
    state_sum(ost, 0, c2, part_got2, s2)
    norm_into(s2, mgain, u2, 0)
    send_u2s = to_mate(u2.at[pl.ds(0, rows)], u2.at[pl.ds(rows, rows)], 5)
    send_u2s.start()
    send_u2s.wait_recv()
    project(u2, 0)

    @pl.when(layer > 0)
    def _():
        token_copy(up).wait_recv()

    @pl.when(layer == 0)
    def _():
        x2[:, 0:chunk] = emb_red[...]

        @pl.loop(1, n_layers)
        def _(i):
            cols = pl.ds(pl.multiple_of(i * chunk, chunk), chunk)
            pltpu.make_async_remote_copy(
                src_ref=emb_red,
                dst_ref=x2.at[:, cols],
                send_sem=red_send,
                recv_sem=red_recv.at[i],
                device_id={"section": mate},
                device_id_type=MESH,
            ).wait_recv()

    norm_into(x2, wgain, u2, 2 * rows)
    send_u2t = to_mate(u2.at[pl.ds(2 * rows, rows)], u2.at[pl.ds(3 * rows, rows)], 6)
    send_u2t.start()
    send_u2t.wait_recv()
    project(u2, 2 * rows)

    attend(o2, 2 * rows, True)
    back(o2, 3 * rows, part_send3)
    send_p3 = to_mate(part_send3, part_got3, 7)
    send_p3.start()
    attend(o2, 0, False)
    back(o2, rows, part_send4)
    send_p4 = to_mate(part_send4, part_got4, 8)
    send_p4.start()
    send_p3.wait_recv()
    token_sum(o2, 2 * rows, x2, part_got3, fin_tok)
    write_tok = pltpu.make_async_copy(fin_tok, tok_out, out_sem.at[0])
    write_tok.start()
    send_p4.wait_recv()
    state_sum(o2, 0, s2, part_got4, fin_st)
    write_st = pltpu.make_async_copy(fin_st, st_out, out_sem.at[1])
    write_st.start()

    for copy in (
        send_u1s,
        send_u1t,
        send_c,
        send_emb,
        send_p1,
        send_o,
        send_p2,
        send_u2s,
        send_u2t,
        send_p3,
        send_p4,
    ):
        copy.wait_send()

    @pl.loop(1, n_layers)
    def _(step):
        a2a_copy(step).wait_send()

    @pl.when(layer < last)
    def _():
        token_copy(up).wait_send()

    @pl.when(layer > 0)
    def _():
        red_copy().wait_send()

    write_tok.wait()
    write_st.wait()


def per_device(n_layers, n_seg, codes, table, tok, st, wq, wk, wv, wo, wgain, mgain, keep, scale):
    rows, width = tok.shape[1:]
    inner = wq.shape[2]
    vocab = table.shape[0]
    chunk = width // n_layers
    any_spec = pl.BlockSpec(memory_space=pl.ANY)
    act = pltpu.VMEM((rows, width), BF16)
    big = pltpu.VMEM((4 * rows, width), BF16)
    mid = pltpu.VMEM((4 * rows, inner), BF16)
    emb = pltpu.VMEM((n_layers, rows, chunk), BF16)
    gain = pltpu.VMEM(wgain.shape, F32)
    sem = pltpu.SemaphoreType.DMA
    tok_new, st_new = pl.pallas_call(
        functools.partial(cell_kernel, n_layers, n_seg),
        out_shape=(jax.ShapeDtypeStruct((rows, width), BF16),) * 2,
        in_specs=[any_spec] * 11 + [pl.BlockSpec(memory_space=pltpu.SMEM)],
        out_specs=(any_spec, any_spec),
        scratch_shapes=[
            pltpu.VMEM(codes.shape, jnp.int32),
            pltpu.VMEM((vocab, width), BF16),
            act,
            act,
            pltpu.VMEM((width, inner), BF16),
            pltpu.VMEM((width, inner), BF16),
            pltpu.VMEM((width, inner), BF16),
            pltpu.VMEM((inner, width), BF16),
            gain,
            gain,
            gain,
            pltpu.VMEM((codes.shape[1], vocab), BF16),
            emb,
            emb,
            emb,
            emb,
            pltpu.VMEM((rows, chunk), BF16),
            big,
            big,
            mid,
            mid,
            mid,
            mid,
            mid,
            pltpu.VMEM((2 * rows, inner), BF16),
        ]
        + [act] * 14
        + [
            sem((11,)),
            sem((9,)),
            sem((9,)),
            sem((n_layers,)),
            sem((n_layers,)),
            sem,
            sem((n_layers,)),
            sem((2,)),
            sem((2,)),
            sem,
            sem,
            sem((2,)),
        ],
        compiler_params=pltpu.CompilerParams(
            collective_id=0, has_side_effects=True, vmem_limit_bytes=58 * 1024 * 1024
        ),
    )(
        codes,
        table,
        tok[0],
        st[0],
        wq[0],
        wk[0],
        wv[0],
        wo[0],
        wgain,
        mgain,
        keep,
        scale,
    )
    return (tok_new[None], st_new[None])


def solution(mesh):
    placed = (
        P("seg", None),
        P("section", None),
        P("seg", "section", None),
        P("seg", "section", None),
        P("section", None, None),
        P("section", None, None),
        P("section", None, None),
        P("section", None, None),
        P(),
        P(),
        P(),
        P("section", None),
    )
    return jax.shard_map(
        functools.partial(per_device, mesh.shape["section"] // 2, mesh.shape["seg"]),
        mesh=mesh,
        in_specs=placed,
        out_specs=(P("seg", "section", None), P("seg", "section", None)),
        check_vma=False,
    )
```

time: 154 us -> 58 us (0.38)
  blocking collectives: 79.4 us -> 0 us
  Pallas kernels: 0 us -> 53.4 us
  matrix products: 33.1 us -> 0 us
  other arithmetic: 15.9 us -> 0 us
  waiting for transfers between devices: 11 us -> 0 us
  starting transfers between devices: 8.86 us -> 0 us
    psum x1 -> x0, blocking collectives: 79.4 us -> none  [per_device(): embedded = lax.psum(looked, 'section').astype(jnp.bfloat16)]
    pallas_call x0 -> x1, Pallas kernels: none -> 53.4 us  [per_device(): pl.pallas_call(functools.partial(cell_kernel, n_layers, n_seg), out_shape...]
    dot_general x11 -> x0, matrix products: 23.4 us -> none  [the longest x2 5.62 us: head_partial(): jnp.einsum('hqk,khd->qhd', weights, value_rows, preferred_element_type=jn...]
    ppermute x10 -> x0, waiting for transfers between devices: 11 us -> none  [the longest x1 7.34 us: passed_along(): return lax.ppermute(block, axis, route)]
    sub x2 -> x0, matrix products: 9.72 us -> none  [head_partial(): exponent = jnp.exp(masked - row_peak)]
    ppermute x10 -> x0, starting transfers between devices: 8.86 us -> none  [the longest x1 5.62 us: from_behind(): lax.ppermute(value, axis, [(source, source + steps) for source in range(i...]
    convert_element_type x5 -> x0, other arithmetic: 7.68 us -> none  [the longest x4 4.64 us: norm_rows(): return (wide * lax.rsqrt(meansq + 1e-06) * gain_row).astype(jnp.bfloat16)]
    reduce_sum x3 -> x0, other arithmetic: 3.79 us -> none  [norm_rows(): meansq = jnp.mean(wide * wide, axis=-1, keepdims=True)]
  transfers between devices with their start and end apart: 10 -> 0, of which waited for: 4 -> 0; matrix products, arithmetic and copies ran while one was open for 5% -> 0% of each run, Pallas kernels for 0% -> 0%
where the time goes in v1:
time: 58 us; the launch traced here: 57.8 us
  Pallas kernels  53.4 us (92%)
  local copies, waits for them, and re-layouts  3.76 us (6%)
  between operations  0.64 us (1%)
    pallas_call x1, Pallas kernels, per_device(): pl.pallas_call(functools.partial(cell_kernel, n_layers, n_seg), out_shape...  53.4 us
    unnamed x2, local copies, waits for them, and re-layouts  3.76 us

profile of v1, /device:TPU:0, one launch (start us, length us, event | category | flops | bytes accessed | tf_op | source)
XLA Modules:
  0.0 57.8 jit_solution(281096975824745803)
XLA Ops:
  0.6 53.4 %shard_map.131 = (bf16[128,2048]{1,0:T(8,128)(2,1)}, bf16[128,2048]{1,0:T(8,128)(2,1)}) custom-call(s32[1,256]{1,0:T(1,128)} %codes_hbm.1, bf16[1024,2048]{1,0:T(8,128)(2,1)} %table_hbm.1, bf16[128,2048]{1,0:T(8,128)(2,1)} %bitcast.12, bf16[128,2048]{1,0:T(8,128)(2,1)} %bitcast.13, bf16[2048,512]{1,0:T(8,128)(2,1)} %bitcast.8, bf16[2048,512]{1,0:T(8,128)(2,1)} %bitcast.9, ...), custom_call_target="tpu_custom_call" | custom-call | tf_op jit(solution)/shard_map/pallas_call | solution.py:447
  54.0 1.9 %copy.16 = bf16[1,128,2048]{2,1,0:T(8,128)(2,1)} copy(bf16[1,128,2048]{2,1,0:T(8,128)(2,1)} %bitcast.15) | data formatting | bytes 1048576
  55.9 1.9 %copy.17 = bf16[1,128,2048]{2,1,0:T(8,128)(2,1)} copy(bf16[1,128,2048]{2,1,0:T(8,128)(2,1)} %bitcast.14) | data formatting | bytes 1048576

commit v2 on v1

--- a/solution.py
+++ b/solution.py
@@ -61,19 +61,25 @@
     c2,
     y1,
     s2,
-    part_send1,
-    part_got1,
-    part_send2,
-    part_got2,
-    part_send3,
-    part_got3,
-    part_send4,
-    part_got4,
+    send_a,
+    got_a,
+    send_b,
+    got_b,
+    send_c_part,
+    got_c_part,
+    send_d,
+    got_d,
     fin_tok,
     fin_st,
+    kept_a,
+    kept_b,
+    kept_c,
+    kept_d,
     load_sem,
     pair_send,
     pair_recv,
+    part_ssem,
+    part_rsem,
     a2a_send,
     a2a_recv,
     red_send,
@@ -95,6 +101,8 @@
     width = x1.shape[1]
     chunk = width // n_layers
     heads = wq.shape[1] // HEAD_DIM
+    kept = (kept_a, kept_b, kept_c, kept_d)
+    parts = ((send_a, got_a), (send_b, got_b), (send_c_part, got_c_part), (send_d, got_d))
 
     barrier = pltpu.get_barrier_semaphore()
     pl.semaphore_signal(barrier, inc=1, device_id={"section": mate}, device_id_type=MESH)
@@ -120,15 +128,15 @@
         (wo_hbm, wo),
     )
     loads = [pltpu.make_async_copy(a, b, load_sem.at[i]) for i, (a, b) in enumerate(pairs)]
-    for load in loads:
+    for load in loads[:6]:
         load.start()
 
-    def norm_into(src, gain_ref, dst, base):
+    def norm_into(src, gain_ref, dst, base, first=0, count=rows):
         gain = gain_ref[pl.ds(layer, 1), :]
 
-        @pl.loop(0, rows // 16)
+        @pl.loop(0, count // 16)
         def _(i):
-            r = pl.multiple_of(i * 16, 16)
+            r = pl.multiple_of(first + i * 16, 16)
             wide = src[pl.ds(r, 16), :].astype(F32)
             meansq = jnp.mean(wide * wide, axis=-1, keepdims=True)
             dst[pl.ds(base + r, 16), :] = (wide * lax.rsqrt(meansq + 1e-06) * gain).astype(BF16)
@@ -160,70 +168,89 @@
                 block, w[...], preferred_element_type=F32
             ).astype(BF16)
 
-    def attend(o, first, masked):
-        @pl.loop(0, 2)
-        def _(b):
-            base = pl.multiple_of(first + b * rows, rows)
+    def attend(o, first, masked, some=tuple(range(heads))):
+        block = pl.ds(first, 2 * rows)
+        if masked:
+            col = lax.broadcasted_iota(jnp.int32, (1, 4 * rows), 1)
+            row = lax.broadcasted_iota(jnp.int32, (2 * rows, 1), 0)
+            own = half * rows
+            far = (1 - half) * rows
+            kpos = jnp.where(
+                col < 2 * rows,
+                -1,
+                jnp.where(col < 3 * rows, col - 2 * rows + own, col - 3 * rows + far),
+            )
+            qpos = jnp.where(row < rows, row + own, row - rows + far)
+        for h in some:
+            lanes = pl.ds(h * HEAD_DIM, HEAD_DIM)
+            s = lax.dot_general(
+                q[block, lanes],
+                k[:, lanes],
+                (((1,), (1,)), ((), ())),
+                preferred_element_type=F32,
+            )
+            s = s * (scale_ref[0, h] * (LOG2E / math.sqrt(HEAD_DIM)))
             if masked:
-                col = lax.broadcasted_iota(jnp.int32, (rows, 4 * rows), 1)
-                row = lax.broadcasted_iota(jnp.int32, (rows, 4 * rows), 0)
-                own = half * rows
-                far = (1 - half) * rows
-                kpos = jnp.where(
-                    col < 2 * rows,
-                    -1,
-                    jnp.where(col < 3 * rows, col - 2 * rows + own, col - 3 * rows + far),
-                )
-                qpos = row + (own + b * (far - own))
-                allowed = kpos <= qpos
-            for h in range(heads):
-                lanes = pl.ds(h * HEAD_DIM, HEAD_DIM)
-                s = lax.dot_general(
-                    q[pl.ds(base, rows), lanes],
-                    k[:, lanes],
-                    (((1,), (1,)), ((), ())),
-                    preferred_element_type=F32,
-                )
-                s = s * (scale_ref[0, h] * (LOG2E / math.sqrt(HEAD_DIM)))
-                if masked:
-                    s = jnp.where(allowed, s, -jnp.inf)
-                e = jnp.exp2(s - jnp.max(s, axis=-1, keepdims=True))
-                p = (e * (1.0 / jnp.sum(e, axis=-1, keepdims=True))).astype(BF16)
-                o[pl.ds(base, rows), lanes] = jnp.dot(
-                    p, v[:, lanes], preferred_element_type=F32
-                ).astype(BF16)
-
-    def back(o, base, dst):
-        dst[...] = jnp.dot(
-            o[pl.ds(base, rows), :], wo[...], preferred_element_type=F32
-        ).astype(BF16)
-
-    def token_sum(o, base, x, got, dst):
-        @pl.loop(0, width // 512)
+                s = jnp.where(kpos <= qpos, s, -jnp.inf)
+            e = jnp.exp2(s - jnp.max(s, axis=-1, keepdims=True))
+            p = (e * (1.0 / jnp.sum(e, axis=-1, keepdims=True))).astype(BF16)
+            o[block, lanes] = jnp.dot(p, v[:, lanes], preferred_element_type=F32).astype(BF16)
+
+    tiles = 4
+    span = width // tiles
+
+    def part_copy(which, t):
+        send, got = parts[which]
+        cols = pl.ds(pl.multiple_of(t * span, span), span)
+        return pltpu.make_async_remote_copy(
+            src_ref=send.at[:, cols],
+            dst_ref=got.at[:, cols],
+            send_sem=part_ssem.at[which * tiles + t],
+            recv_sem=part_rsem.at[which * tiles + t],
+            device_id={"section": mate},
+            device_id_type=MESH,
+        )
+
+    def back(o, base, which):
+        @pl.loop(0, tiles)
         def _(t):
-            cols = pl.ds(pl.multiple_of(t * 512, 512), 512)
-            mine = jnp.dot(
-                o[pl.ds(base, rows), :], wo[:, cols], preferred_element_type=F32
+            cols = pl.ds(pl.multiple_of(t * span, span), span)
+            both = jnp.dot(
+                o[pl.ds(base, 2 * rows), :], wo[:, cols], preferred_element_type=F32
             ).astype(BF16)
-            total = mine.astype(F32) + got[:, cols].astype(F32)
+            parts[which][0][:, cols] = both[rows:]
+            kept[which][:, cols] = both[:rows]
+            part_copy(which, t).start()
+
+    def summed(which, finish, after=None):
+        @pl.loop(0, tiles)
+        def _(t):
+            cols = pl.ds(pl.multiple_of(t * span, span), span)
+            part_copy(which, t).wait_recv()
+            finish(cols, kept[which][:, cols].astype(F32) + parts[which][1][:, cols].astype(F32))
+            if after is not None:
+                after(t)
+
+    def token_finish(x, dst):
+        def finish(cols, total):
             dst[:, cols] = (x[:, cols].astype(F32) + total).astype(BF16)
 
-    def state_sum(o, base, c, got, dst):
-        @pl.loop(0, width // 512)
-        def _(t):
-            cols = pl.ds(pl.multiple_of(t * 512, 512), 512)
-            mine = jnp.dot(
-                o[pl.ds(base, rows), :], wo[:, cols], preferred_element_type=F32
-            ).astype(BF16)
-            total = mine.astype(F32) + got[:, cols].astype(F32)
+        return finish
+
+    def state_finish(c, dst):
+        def finish(cols, total):
             r = keep[pl.ds(layer, 1), cols]
             dst[:, cols] = (r * c[:, cols].astype(F32) + (1.0 - r) * total).astype(BF16)
 
+        return finish
+
     loads[0].wait()
     loads[2].wait()
-    norm_into(c1, mgain, u1, 0)
     loads[1].wait()
     loads[3].wait()
+    for load in loads[6:]:
+        load.start()
+    norm_into(c1, mgain, u1, 0)
     norm_into(x1, wgain, u1, 2 * rows)
     pl.semaphore_wait(barrier, n_layers + 2)
     send_u1s = to_mate(u1.at[pl.ds(0, rows)], u1.at[pl.ds(rows, rows)], 0)
@@ -294,32 +321,49 @@
 
     attend(o1, 2 * rows, True)
     loads[10].wait()
-    back(o1, 3 * rows, part_send1)
-    send_p1 = to_mate(part_send1, part_got1, 3)
-    send_p1.start()
-    send_p1.wait_recv()
-    token_sum(o1, 2 * rows, x1, part_got1, y1)
-
-    def token_copy(target):
+    back(o1, 2 * rows, 0)
+
+    last = n_layers - 1
+    up = jnp.where(layer < last, pos + 2, pos - 2 * last)
+    upper = rows // 2
+
+    def token_copy(row, cols, i):
         return pltpu.make_async_remote_copy(
-            src_ref=y1,
-            dst_ref=x2,
-            send_sem=tok_send,
-            recv_sem=tok_recv,
-            device_id={"section": target},
+            src_ref=y1.at[pl.ds(row, upper), cols],
+            dst_ref=x2.at[pl.ds(row, upper), cols],
+            send_sem=tok_send.at[i],
+            recv_sem=tok_recv.at[i],
+            device_id={"section": up},
             device_id_type=MESH,
         )
 
-    last = n_layers - 1
-    up = jnp.where(layer < last, pos + 2, pos - 2 * last)
+    def upper_copy(t):
+        return token_copy(0, pl.ds(pl.multiple_of(t * span, span), span), t)
+
+    def lower_copy():
+        return token_copy(upper, pl.ds(0, width), tiles)
+
+    def send_tile(t):
+        @pl.when(layer < last)
+        def _():
+            upper_copy(t).start()
+
+    def send_heads(i):
+        lanes = pl.ds(i * (heads // 2) * HEAD_DIM, (heads // 2) * HEAD_DIM)
+        copy = to_seg(o1.at[pl.ds(0, 2 * rows), lanes], ost.at[:, lanes], 1 + i)
+        copy.start()
+        return copy
+
+    attend(o1, 0, False, range(heads // 2))
+    send_o0 = send_heads(0)
+    summed(0, token_finish(x1, y1), send_tile)
 
     @pl.when(layer < last)
     def _():
-        token_copy(up).start()
-
-    attend(o1, 0, False)
-    send_o = to_seg(o1.at[pl.ds(0, 2 * rows)], ost, 1)
-    send_o.start()
+        lower_copy().start()
+
+    attend(o1, 0, False, range(heads // 2, heads))
+    send_o1 = send_heads(1)
 
     emb_red[...] = emb_own[layer]
 
@@ -344,23 +388,23 @@
     def _():
         red_copy().start()
 
-    send_o.wait_recv()
-    back(ost, rows, part_send2)
-    send_p2 = to_mate(part_send2, part_got2, 4)
-    send_p2.start()
+    send_o0.wait_recv()
+    send_o1.wait_recv()
+    back(ost, 0, 1)
     send_c.wait_recv()
     loads[9].wait()
-    send_p2.wait_recv()
-    state_sum(ost, 0, c2, part_got2, s2)
+    summed(1, state_finish(c2, s2))
     norm_into(s2, mgain, u2, 0)
-    send_u2s = to_mate(u2.at[pl.ds(0, rows)], u2.at[pl.ds(rows, rows)], 5)
+    send_u2s = to_mate(u2.at[pl.ds(0, rows)], u2.at[pl.ds(rows, rows)], 3)
     send_u2s.start()
     send_u2s.wait_recv()
     project(u2, 0)
 
     @pl.when(layer > 0)
     def _():
-        token_copy(up).wait_recv()
+        @pl.loop(0, tiles)
+        def _(t):
+            upper_copy(t).wait_recv()
 
     @pl.when(layer == 0)
     def _():
@@ -378,26 +422,31 @@
                 device_id_type=MESH,
             ).wait_recv()
 
-    norm_into(x2, wgain, u2, 2 * rows)
-    send_u2t = to_mate(u2.at[pl.ds(2 * rows, rows)], u2.at[pl.ds(3 * rows, rows)], 6)
-    send_u2t.start()
-    send_u2t.wait_recv()
+    norm_into(x2, wgain, u2, 2 * rows, 0, upper)
+    send_u2a = to_mate(u2.at[pl.ds(2 * rows, upper)], u2.at[pl.ds(3 * rows, upper)], 4)
+    send_u2a.start()
+
+    @pl.when(layer > 0)
+    def _():
+        lower_copy().wait_recv()
+
+    norm_into(x2, wgain, u2, 2 * rows, upper, upper)
+    send_u2b = to_mate(
+        u2.at[pl.ds(2 * rows + upper, upper)], u2.at[pl.ds(3 * rows + upper, upper)], 5
+    )
+    send_u2b.start()
+    send_u2a.wait_recv()
+    send_u2b.wait_recv()
     project(u2, 2 * rows)
 
     attend(o2, 2 * rows, True)
-    back(o2, 3 * rows, part_send3)
-    send_p3 = to_mate(part_send3, part_got3, 7)
-    send_p3.start()
+    back(o2, 2 * rows, 2)
     attend(o2, 0, False)
-    back(o2, rows, part_send4)
-    send_p4 = to_mate(part_send4, part_got4, 8)
-    send_p4.start()
-    send_p3.wait_recv()
-    token_sum(o2, 2 * rows, x2, part_got3, fin_tok)
+    back(o2, 0, 3)
+    summed(2, token_finish(x2, fin_tok))
     write_tok = pltpu.make_async_copy(fin_tok, tok_out, out_sem.at[0])
     write_tok.start()
-    send_p4.wait_recv()
-    state_sum(o2, 0, s2, part_got4, fin_st)
+    summed(3, state_finish(s2, fin_st))
     write_st = pltpu.make_async_copy(fin_st, st_out, out_sem.at[1])
     write_st.start()
 
@@ -406,13 +455,11 @@
         send_u1t,
         send_c,
         send_emb,
-        send_p1,
-        send_o,
-        send_p2,
+        send_o0,
+        send_o1,
         send_u2s,
-        send_u2t,
-        send_p3,
-        send_p4,
+        send_u2a,
+        send_u2b,
     ):
         copy.wait_send()
 
@@ -420,9 +467,19 @@
     def _(step):
         a2a_copy(step).wait_send()
 
+    for which in range(len(parts)):
+
+        @pl.loop(0, tiles)
+        def _(t, which=which):
+            part_copy(which, t).wait_send()
+
     @pl.when(layer < last)
     def _():
-        token_copy(up).wait_send()
+        @pl.loop(0, tiles)
+        def _(t):
+            upper_copy(t).wait_send()
+
+        lower_copy().wait_send()
 
     @pl.when(layer > 0)
     def _():
@@ -430,6 +487,17 @@
 
     write_tok.wait()
     write_st.wait()
+
+
+def write_kernel(tok_in, st_in, tok_out, st_out, sems):
+    copies = (
+        pltpu.make_async_copy(tok_in, tok_out, sems.at[0]),
+        pltpu.make_async_copy(st_in, st_out, sems.at[1]),
+    )
+    for copy in copies:
+        copy.start()
+    for copy in copies:
+        copy.wait()
 
 
 def per_device(n_layers, n_seg, codes, table, tok, st, wq, wk, wv, wo, wgain, mgain, keep, scale):
@@ -476,19 +544,21 @@
             mid,
             pltpu.VMEM((2 * rows, inner), BF16),
         ]
-        + [act] * 14
+        + [act] * 18
         + [
             sem((11,)),
-            sem((9,)),
-            sem((9,)),
+            sem((6,)),
+            sem((6,)),
+            sem((16,)),
+            sem((16,)),
             sem((n_layers,)),
             sem((n_layers,)),
             sem,
             sem((n_layers,)),
-            sem((2,)),
-            sem((2,)),
-            sem,
-            sem,
+            sem((3,)),
+            sem((3,)),
+            sem((5,)),
+            sem((5,)),
             sem((2,)),
         ],
         compiler_params=pltpu.CompilerParams(
@@ -508,6 +578,13 @@
         keep,
         scale,
     )
+    tok_new, st_new = pl.pallas_call(
+        write_kernel,
+        out_shape=(jax.ShapeDtypeStruct((rows, width), BF16),) * 2,
+        in_specs=[pl.BlockSpec(memory_space=pltpu.VMEM)] * 2,
+        out_specs=(any_spec, any_spec),
+        scratch_shapes=[sem((2,))],
+    )(tok_new, st_new)
     return (tok_new[None], st_new[None])
 
 

time: 58 us -> 48.7 us (0.84); the launches traced: 57.8 us -> 47.9 us
  Pallas kernels: 53.4 us -> 47.3 us
  local copies, waits for them, and re-layouts: 3.76 us -> 0 us
    pallas_call x1, Pallas kernels: 53.4 us -> 45.1 us  [per_device(): pl.pallas_call(functools.partial(cell_kernel, n_layers, n_seg), out_shape...]
    unnamed x2 -> x0, local copies, waits for them, and re-layouts: 3.76 us -> none
    pallas_call x0 -> x1, Pallas kernels: none -> 2.18 us  [per_device(): pl.pallas_call(write_kernel, out_shape=(jax.ShapeDtypeStruct((rows, width...]
where the time goes in v2:
time: 48.7 us; the launch traced here: 47.9 us
  Pallas kernels  47.3 us (97%)
  between operations  0.64 us (1%)
    pallas_call x1, Pallas kernels, per_device(): pl.pallas_call(functools.partial(cell_kernel, n_layers, n_seg), out_shape...  45.1 us
    pallas_call x1, Pallas kernels, per_device(): pl.pallas_call(write_kernel, out_shape=(jax.ShapeDtypeStruct((rows, width...  2.18 us

profile of v2, /device:TPU:0, one launch (start us, length us, event | category | flops | bytes accessed | tf_op | source)
XLA Modules:
  0.0 47.9 jit_solution(17626044916198234504)
XLA Ops:
  0.6 45.1 %shard_map.131 = (bf16[128,2048]{1,0:T(8,128)(2,1)}, bf16[128,2048]{1,0:T(8,128)(2,1)}) custom-call(s32[1,256]{1,0:T(1,128)} %codes_hbm.1, bf16[1024,2048]{1,0:T(8,128)(2,1)} %table_hbm.1, bf16[128,2048]{1,0:T(8,128)(2,1)} %bitcast.12, bf16[128,2048]{1,0:T(8,128)(2,1)} %bitcast.13, bf16[2048,512]{1,0:T(8,128)(2,1)} %bitcast.8, bf16[2048,512]{1,0:T(8,128)(2,1)} %bitcast.9, ...), custom_call_target="tpu_custom_call" | custom-call | tf_op jit(solution)/shard_map/pallas_call | solution.py:515
  45.7 2.2 %shard_map.132 = (bf16[128,2048]{1,0:T(8,128)(2,1)}, bf16[128,2048]{1,0:T(8,128)(2,1)}) custom-call(bf16[128,2048]{1,0:T(8,128)(2,1)} %get-tuple-element.6.tok_in, bf16[128,2048]{1,0:T(8,128)(2,1)} %get-tuple-element.7.st_in), custom_call_target="tpu_custom_call" | custom-call | tf_op jit(solution)/shard_map/pallas_call | solution.py:581

commit v3 on v2

--- a/solution.py
+++ b/solution.py
@@ -489,15 +489,17 @@
     write_st.wait()
 
 
-def write_kernel(tok_in, st_in, tok_out, st_out, sems):
-    copies = (
-        pltpu.make_async_copy(tok_in, tok_out, sems.at[0]),
-        pltpu.make_async_copy(st_in, st_out, sems.at[1]),
-    )
-    for copy in copies:
-        copy.start()
-    for copy in copies:
-        copy.wait()
+def write_kernel(tok_in, st_in, tok_out, st_out, held, in_sems, out_sems):
+    ends = ((tok_in, tok_out), (st_in, st_out))
+    reads = [pltpu.make_async_copy(a, held.at[i], in_sems.at[i]) for i, (a, _) in enumerate(ends)]
+    writes = [pltpu.make_async_copy(held.at[i], b, out_sems.at[i]) for i, (_, b) in enumerate(ends)]
+    for read in reads:
+        read.start()
+    for read, write in zip(reads, writes):
+        read.wait()
+        write.start()
+    for write in writes:
+        write.wait()
 
 
 def per_device(n_layers, n_seg, codes, table, tok, st, wq, wk, wv, wo, wgain, mgain, keep, scale):
@@ -581,9 +583,9 @@
     tok_new, st_new = pl.pallas_call(
         write_kernel,
         out_shape=(jax.ShapeDtypeStruct((rows, width), BF16),) * 2,
-        in_specs=[pl.BlockSpec(memory_space=pltpu.VMEM)] * 2,
+        in_specs=[any_spec, any_spec],
         out_specs=(any_spec, any_spec),
-        scratch_shapes=[sem((2,))],
+        scratch_shapes=[pltpu.VMEM((2, rows, width), BF16), sem((2,)), sem((2,))],
     )(tok_new, st_new)
     return (tok_new[None], st_new[None])
 

time: 48.7 us -> 48.6 us (level)
  no operation moved by 1% of the time
where the time goes in v3:
time: 48.6 us; the launch traced here: 47.8 us
  Pallas kernels  47.1 us (97%)
  between operations  0.64 us (1%)
    pallas_call x1, Pallas kernels, per_device(): pl.pallas_call(functools.partial(cell_kernel, n_layers, n_seg), out_shape...  45.1 us
    pallas_call x1, Pallas kernels, per_device(): pl.pallas_call(write_kernel, out_shape=(jax.ShapeDtypeStruct((rows, width...  2.04 us

profile of v3, /device:TPU:0, one launch (start us, length us, event | category | flops | bytes accessed | tf_op | source)
XLA Modules:
  0.0 47.8 jit_solution(3181681566386740509)
XLA Ops:
  0.6 45.1 %shard_map.131 = (bf16[128,2048]{1,0:T(8,128)(2,1)}, bf16[128,2048]{1,0:T(8,128)(2,1)}) custom-call(s32[1,256]{1,0:T(1,128)} %codes_hbm.1, bf16[1024,2048]{1,0:T(8,128)(2,1)} %table_hbm.1, bf16[128,2048]{1,0:T(8,128)(2,1)} %bitcast.12, bf16[128,2048]{1,0:T(8,128)(2,1)} %bitcast.13, bf16[2048,512]{1,0:T(8,128)(2,1)} %bitcast.8, bf16[2048,512]{1,0:T(8,128)(2,1)} %bitcast.9, ...), custom_call_target="tpu_custom_call" | custom-call | tf_op jit(solution)/shard_map/pallas_call | solution.py:517
  45.7 2.0 %shard_map.132 = (bf16[128,2048]{1,0:T(8,128)(2,1)}, bf16[128,2048]{1,0:T(8,128)(2,1)}) custom-call(bf16[128,2048]{1,0:T(8,128)(2,1)} %get-tuple-element.6.tok_in, bf16[128,2048]{1,0:T(8,128)(2,1)} %get-tuple-element.7.st_in), custom_call_target="tpu_custom_call" | custom-call | tf_op jit(solution)/shard_map/pallas_call | solution.py:583
